TPU v7x, 32 devices: a whole 2x2x4 slice. The times are simulated.
32 devices in a mesh: groups: 2 (over x), wide: 16 (over z, y, core).
Axes of the slice: x: 2, y: 2, z: 4, core: 2. Of those that a mesh axis runs over, the one named last changes fastest.
Arguments:
- plus_counts: int32 [8192, 8, 2048], P(('groups', 'wide')), parts along dimension 0, may hold values from 32 to 160
- report_counts: int32 [8192, 8, 2048], P(('groups', 'wide')), parts along dimension 0, may hold values from 128 to 256
- clip_bounds: int32 [8192, 8], P(('groups', 'wide')), parts along dimension 0, may hold values from 16 to 159
Outputs:
- histogram: float32 [8192, 8, 2048], P(('groups', 'wide')), parts along dimension 0
There are 2 independent parts, one for each index of `groups`. A program takes and returns all parts, laid end to end along the dimension named above; each array names one. Nothing has to cross between parts.
All inputs are finite; a program needn't handle non-finite values.
Results may differ from a plain program's by a relative error of at most 0.0041.
Values may be sent and summed in bfloat16 or wider, within the bound.
A program may use at most 320 MiB of HBM per device.

v0:
```python
import jax
import jax.numpy as jnp
from jax import lax
from jax.sharding import PartitionSpec as P


def sylvester(order):
    idx = jnp.arange(order, dtype=jnp.int32)
    both = jnp.bitwise_and(idx[:, None], idx[None, :])
    parity = jnp.zeros((order, order), jnp.int32)
    for shift_bit in range(max(order.bit_length() - 1, 1)):
        parity = parity + jnp.bitwise_and(jnp.right_shift(both, shift_bit), 1)
    return 1.0 - 2.0 * jnp.bitwise_and(parity, 1).astype(jnp.float32)


def kron_hadamard(order):
    left_order = 64 if order >= 4096 else max(order // 64, 1)
    right_order = order // left_order
    left = sylvester(left_order).astype(jnp.bfloat16)
    right = sylvester(right_order).astype(jnp.bfloat16)
    return (left[:, None, :, None] * right[None, :, None, :]).reshape(order, order)


def shards(plus_counts, report_counts, clip_bounds):
    rows_local, middle, trailing = plus_counts.shape
    bound = clip_bounds[:, :, None]
    numer = jnp.clip(2 * plus_counts - report_counts, -bound, bound).astype(jnp.float32)
    residual = (numer / report_counts.astype(jnp.float32)).astype(jnp.bfloat16)
    hadamard_b = kron_hadamard(trailing)
    hadamard_c = sylvester(middle)
    inner = jnp.dot(
        residual.reshape(rows_local * middle, trailing),
        hadamard_b,
        preferred_element_type=jnp.float32,
    )
    inner = jnp.einsum(
        "dc,acb->adb",
        hadamard_c,
        inner.reshape(rows_local, middle, trailing),
        precision=lax.Precision.HIGHEST,
    )
    mixed = (inner * (1.0 / 128.0)).astype(jnp.bfloat16)
    leading = rows_local * lax.axis_size("wide")
    hadamard_a = kron_hadamard(leading)
    regrouped = lax.all_to_all(mixed, "wide", split_axis=2, concat_axis=0, tiled=True)
    width_mid = regrouped.shape[1]
    outer = jnp.dot(hadamard_a, regrouped.reshape(leading, -1), preferred_element_type=jnp.float32)
    decoded = (outer * (1.0 / 64.0)).reshape(leading, width_mid, -1)
    histogram = lax.all_to_all(decoded, "wide", split_axis=0, concat_axis=2, tiled=True)
    return histogram


def solution(mesh):
    placed = (
        P(("groups", "wide"), None, None),
        P(("groups", "wide"), None, None),
        P(("groups", "wide"), None),
    )
    return jax.shard_map(
        shards,
        mesh=mesh,
        in_specs=placed,
        out_specs=P(("groups", "wide"), None, None),
        check_vma=False,
    )
```

profile of v0, /device:TPU:1, one launch (start us, length us, event | category | flops | bytes accessed | tf_op | source)
XLA Modules:
  0.0 734.2 jit_solution(3613008291054733877)
XLA Ops:
  0.1 0.7 neg.4
  0.8 0.8 copy.17
  1.6 6.1 broadcast_multiply_fusion.1
  7.7 23.5 %reshape.135 = bf16[2048,2048,1]{1,0,2:T(8,128)(2,1)} reshape(bf16[32,64,32,64]{3,2,1,0:T(8,128)(2,1)} %broadcast_multiply_fusion.1) | data formatting | bytes 16777216 | tf_op jit(solution)/shard_map/mul | solution.py:21
  31.2 0.1 copy.18
  31.3 32.2 %fusion.3 = f32[256,8,2048]{2,1,0:T(8,128)} fusion(bf16[2048,2048,1]{1,0,2:T(8,128)(2,1)} %reshape.135, s32[256,8,2048]{2,1,0:T(8,128)} %param.4, s32[256,8,2048]{2,1,0:T(8,128)} %param.3, s32[256,8]{1,0:T(8,128)S(1)} %copy.18, s32[256,8]{1,0:T(8,128)S(1)} %copy.17), kind=kOutput, calls=%fused_computation.9 | convolution fusion | flops 17213423616 | bytes 58736640 | tf_op jit(solution)/shard_map/dot_general | solution.py:31
  63.5 21.0 %fusion = bf16[256,8,2048]{2,1,0:T(8,128)(2,1)} fusion(f32[256,8,2048]{2,1,0:T(8,128)} %fusion.3), kind=kOutput, calls=%fused_computation.5 | convolution fusion | flops 411042624 | bytes 25165824 | tf_op jit(solution)/shard_map/dc,acb->adb/dot_general | solution.py:36
  84.4 13.3 %copy.19 = bf16[256,8,2048]{0,1,2:T(8,128)(2,1)} copy(bf16[256,8,2048]{2,1,0:T(8,128)(2,1)} %fusion) | data formatting | bytes 16777216 | tf_op jit(solution)/shard_map/convert_element_type | solution.py:42
  97.8 7.4 %all-to-all-start = ((bf16[256,8,2048]{0,1,2:T(8,128)(2,1)}), bf16[256,8,2048]{0,1,2:T(8,128)(2,1)}, u32[]{:S(2)}, u32[]{:S(2)}) async-start(bf16[256,8,2048]{0,1,2:T(8,128)(2,1)} %copy.19), calls=%async_computation | async-start | bytes 16777216 | tf_op jit(solution)/shard_map/all_to_all | solution.py:45
  105.1 21.0 %broadcast_multiply_fusion = bf16[64,64,64,64]{3,2,1,0:T(8,128)(2,1)} fusion(bf16[64,64]{1,0:T(8,128)(2,1)S(1)} %subtract_convert_fusion), kind=kLoop, calls=%fused_computation | loop fusion | flops 16777216 | bytes 33562624 | tf_op jit(solution)/shard_map/mul | solution.py:21
  126.2 86.6 %mul.96 = bf16[4096,4096]{1,0:T(8,128)(2,1)} reshape(bf16[64,64,64,64]{3,2,1,0:T(8,128)(2,1)} %broadcast_multiply_fusion) | data formatting | bytes 67108864 | tf_op jit(solution)/shard_map/mul | solution.py:21
  212.8 43.4 %all-to-all-done = bf16[256,8,2048]{0,1,2:T(8,128)(2,1)} async-done(((bf16[256,8,2048]{0,1,2:T(8,128)(2,1)}), bf16[256,8,2048]{0,1,2:T(8,128)(2,1)}, u32[]{:S(2)}, u32[]{:S(2)}) %all-to-all-start) | async-done | bytes 8388640 | tf_op jit(solution)/shard_map/all_to_all | solution.py:45
  256.2 13.2 %copy.20 = bf16[256,8,16,128]{3,1,0,2:T(8,128)(2,1)} copy(bf16[256,8,16,128]{0,1,3,2:T(8,128)(2,1)} %bitcast.2) | data formatting | bytes 16777216 | tf_op jit(solution)/shard_map/all_to_all | solution.py:45
  269.4 42.4 %convolution_multiply_fusion = f32[4096,1024]{0,1:T(8,128)} fusion(bf16[4096,4096]{1,0:T(8,128)(2,1)} %mul.96, bf16[512,8,8,128]{3,2,1,0:T(8,128)(2,1)} %bitcast.28), kind=kOutput, calls=%fused_computation.4 | convolution fusion | flops 34363932672 | bytes 58720256 | tf_op jit(solution)/shard_map/dot_general | solution.py:47
  311.8 17.5 %copy.21 = f32[4096,8,128]{2,1,0:T(8,128)} copy(f32[4096,8,128]{0,2,1:T(8,128)} %bitcast.27) | data formatting | bytes 33554432 | tf_op jit(solution)/shard_map/reshape | solution.py:48
  329.3 398.4 %all_to_all.33 = f32[4096,8,128]{2,1,0:T(8,128)S(1)} all-to-all(f32[4096,8,128]{2,1,0:T(8,128)} %copy.21), channel_id=1, replica_groups=mesh['groups'=2,'wide'=16] {'wide'}, dimensions={0} | all-to-all | bytes 33554432 | tf_op jit(solution)/shard_map/all_to_all | solution.py:49
  727.7 6.5 copy.29
  (2 shorter events, 0.1 us)
Async XLA Ops:
  97.8 158.5 %all-to-all-start = ((bf16[256,8,2048]{0,1,2:T(8,128)(2,1)}), bf16[256,8,2048]{0,1,2:T(8,128)(2,1)}, u32[]{:S(2)}, u32[]{:S(2)}) async-start(bf16[256,8,2048]{0,1,2:T(8,128)(2,1)} %copy.19), calls=%async_computation | async-start | bytes 16777216 | tf_op jit(solution)/shard_map/all_to_all | solution.py:45
where the time goes:
time: 738 us; the launch traced here: 734 us
  blocking collectives  398 us (54%)
  local copies, waits for them, and re-layouts  162 us (22%)
  matrix products  95.5 us (13%)
  waiting for transfers between devices  43.4 us (6%)
  other arithmetic  27.9 us (4%)
    all_to_all x1, blocking collectives, shards(): lax.all_to_all(decoded, 'wide', split_axis=0, concat_axis=2, tiled=True)  398 us
    mul x2, local copies, waits for them, and re-layouts, kron_hadamard(): left[:, None, :, None] * right[None, :, None, :]  110 us
    all_to_all x1, waiting for transfers between devices, shards(): lax.all_to_all(mixed, 'wide', split_axis=2, concat_axis=0, tiled=True)  43.4 us
    dot_general x1, matrix products, shards(): jnp.dot(hadamard_a, regrouped.reshape(leading, -1), preferred_element_typ...  42.4 us
    dot_general x1, matrix products, shards(): jnp.dot(residual.reshape(rows_local * middle, trailing), hadamard_b, pref...  32.2 us
    mul x2, other arithmetic, kron_hadamard(): left[:, None, :, None] * right[None, :, None, :]  27.2 us
    dot_general x1, matrix products, shards(): jnp.einsum('dc,acb->adb', hadamard_c, inner.reshape(rows_local, middle, t...  21 us
    reshape x1, local copies, waits for them, and re-layouts, shards(): decoded = (outer * (1.0 / 64.0)).reshape(leading, width_mid, -1)  17.5 us
  transfers between devices with their start and end apart: 1, of which 1 were waited for; matrix products, arithmetic and copies ran while one was open for 15% of the time, Pallas kernels for 0%

commit v1 on v0

v1 whole, which is shorter than its diff:
```python
import functools

import jax
import jax.numpy as jnp
from jax import lax
from jax.experimental import pallas as pl
from jax.experimental.pallas import tpu as pltpu
from jax.sharding import PartitionSpec as P

CHUNK = 32
PAIR = 2
FACTOR = 256
LANES = 128
RADIX = 16
MESH = pl.DeviceIdType.MESH


def butterfly(parts):
    parts = list(parts)
    half = 1
    while half < len(parts):
        for low in range(len(parts)):
            if not low & half:
                first, second = parts[low], parts[low | half]
                parts[low], parts[low | half] = first + second, first - second
        half *= 2
    return parts


def signs(both):
    for shift in (8, 4, 2, 1):
        both = both ^ (both >> shift)
    return (1 - 2 * (both & 1)).astype(jnp.float32)


def exchange(
    n, plus_ref, report_ref, bound_ref, out_ref,
    had_b, had_c, plus_buf, report_buf, inner, mixed, got, summed,
    load_sem, send_one, recv_one, send_two, recv_two, own_sem,
):
    me = lax.axis_index("wide")
    chunks, tall, trailing = plus_ref.shape
    middle = tall // CHUNK
    per_group, width = mixed.shape[2], mixed.shape[4]
    blocks = trailing // FACTOR

    def loads(k):
        slot = lax.rem(k, 2)
        return (
            pltpu.make_async_copy(plus_ref.at[k], plus_buf.at[slot], load_sem.at[0, slot]),
            pltpu.make_async_copy(report_ref.at[k], report_buf.at[slot], load_sem.at[1, slot]),
        )

    for load in loads(0):
        load.start()

    barrier = pltpu.get_barrier_semaphore()

    def greet(step, carry):
        pl.semaphore_signal(barrier, inc=1, device_id={"wide": lax.rem(me + step, n)}, device_id_type=MESH)
        return carry

    lax.fori_loop(1, n, greet, 0)

    row = lax.broadcasted_iota(jnp.int32, (FACTOR, FACTOR), 0)
    col = lax.broadcasted_iota(jnp.int32, (FACTOR, FACTOR), 1)
    had_b[...] = signs(row & col).astype(jnp.bfloat16)
    row = lax.broadcasted_iota(jnp.int32, (tall, tall), 0)
    col = lax.broadcasted_iota(jnp.int32, (tall, tall), 1)
    near = (row ^ col) < middle
    had_c[...] = jnp.where(near, signs(row & col & (middle - 1)), 0.0).astype(jnp.bfloat16)

    pl.semaphore_wait(barrier, n - 1)

    def front(k, carry):
        slot = lax.rem(k, 2)

        @pl.when(k + 1 < chunks)
        def _():
            for load in loads(k + 1):
                load.start()

        for load in loads(k):
            load.wait()
        bounds = bound_ref[pl.ds(pl.multiple_of(k * CHUNK, CHUNK), CHUNK), :]
        bounds = jnp.broadcast_to(bounds[:, None, :], (CHUNK, middle, middle)).reshape(tall, middle)
        pick = lax.broadcasted_iota(jnp.int32, (tall, middle), 0) % middle
        pick = pick == lax.broadcasted_iota(jnp.int32, (tall, middle), 1)
        bound = jnp.sum(jnp.where(pick, bounds.astype(jnp.float32), 0.0), axis=1, keepdims=True)
        for block in range(blocks):
            cols = pl.ds(block * FACTOR, FACTOR)
            plus = plus_buf[slot, :, cols]
            report = report_buf[slot, :, cols]
            numer = jnp.clip((2 * plus - report).astype(jnp.float32), -bound, bound)
            residual = (numer / report.astype(jnp.float32)).astype(jnp.bfloat16)
            inner[:, cols] = jnp.dot(residual, had_b[...], preferred_element_type=jnp.float32)

        def across(strip, carry):
            rows = pl.ds(pl.multiple_of(strip * 8, 8), 8)
            parts = butterfly([inner[rows, pl.ds(b * FACTOR, FACTOR)] for b in range(blocks)])
            for b in range(blocks):
                inner[rows, pl.ds(b * FACTOR, FACTOR)] = parts[b]
            return carry

        lax.fori_loop(0, tall // 8, across, 0)
        for block in range(blocks):
            whole = inner[:, pl.ds(block * FACTOR, FACTOR)]
            high = whole.astype(jnp.bfloat16)
            low = (whole - high.astype(jnp.float32)).astype(jnp.bfloat16)
            done = jnp.dot(had_c[...], high, preferred_element_type=jnp.float32)
            done = done + jnp.dot(had_c[...], low, preferred_element_type=jnp.float32)
            done = (done * (1.0 / 128.0)).astype(jnp.bfloat16)
            part, start = divmod(block * FACTOR, width)
            mixed[k, :, part, :, pl.ds(start, FACTOR)] = done.reshape(-1, PAIR * middle, FACTOR)
        got[k, 0] = mixed[k, lax.div(me, per_group), lax.rem(me, per_group)]

        def send(step, carry):
            to = lax.rem(me + step, n)
            pltpu.make_async_remote_copy(
                src_ref=mixed.at[k, lax.div(to, per_group), lax.rem(to, per_group)],
                dst_ref=got.at[k, step],
                send_sem=send_one.at[k],
                recv_sem=recv_one.at[k],
                device_id={"wide": to},
                device_id_type=MESH,
            ).start()
            return carry

        lax.fori_loop(1, n, send, 0)
        return carry

    lax.fori_loop(0, chunks, front, 0)

    def wait_all(k, sem):
        others = got.at[k, pl.ds(1, n - 1)]
        pltpu.make_async_copy(others, others, sem.at[k]).wait()

    def own(k):
        return pltpu.make_async_copy(
            summed.at[k, me], out_ref.at[k, lax.div(me, per_group), lax.rem(me, per_group)], own_sem.at[k]
        )

    def combine(k, carry):
        wait_all(k, recv_one)

        def strip(tile, carry):
            cols = pl.ds(pl.multiple_of(tile * LANES, LANES), LANES)
            parts = [got[k, lax.rem(me + (n - source), n), :, cols].astype(jnp.float32) for source in range(n)]
            parts = butterfly(parts)
            for to in range(n):
                summed[k, to, :, cols] = (parts[to] * (1.0 / 64.0)).astype(jnp.bfloat16)
            return carry

        lax.fori_loop(0, width // LANES, strip, 0)
        own(k).start()

        def send(step, carry):
            to = lax.rem(me + step, n)
            pltpu.make_async_remote_copy(
                src_ref=summed.at[k, to],
                dst_ref=out_ref.at[k, lax.div(me, per_group), lax.rem(me, per_group)],
                send_sem=send_two.at[k],
                recv_sem=recv_two.at[k],
                device_id={"wide": to},
                device_id_type=MESH,
            ).start()
            return carry

        lax.fori_loop(1, n, send, 0)
        return carry

    lax.fori_loop(0, chunks, combine, 0)

    def finish(k, carry):
        own(k).wait()
        wait_all(k, send_one)
        wait_all(k, send_two)
        wait_all(k, recv_two)
        return carry

    lax.fori_loop(0, chunks, finish, 0)


def leading(summed_ref, out_ref):
    rows, middle, wide = out_ref.shape
    chunks, groups = summed_ref.shape[:2]
    tiles = wide // LANES
    per_chunk = CHUNK // RADIX

    def inside(index, carry):
        block, tile = index // tiles, index % tiles
        cols = pl.ds(pl.multiple_of(tile * LANES, LANES), LANES)
        group = pl.ds((block % per_chunk) * (RADIX // PAIR), RADIX // PAIR)
        parts = summed_ref[block // per_chunk, group, 0, :, cols].astype(jnp.float32)
        parts = parts.reshape(RADIX, middle, LANES)
        parts = butterfly([parts[i] for i in range(RADIX)])
        for i in range(RADIX):
            out_ref[block * RADIX + i, :, cols] = parts[i]
        return carry

    lax.fori_loop(0, rows // RADIX * tiles, inside, 0)

    def across(index, carry):
        low, tile = index // tiles, index % tiles
        cols = pl.ds(pl.multiple_of(tile * LANES, LANES), LANES)
        parts = butterfly([out_ref[high * RADIX + low, :, cols] for high in range(rows // RADIX)])
        for high in range(rows // RADIX):
            out_ref[high * RADIX + low, :, cols] = parts[high]
        return carry

    lax.fori_loop(0, RADIX * tiles, across, 0)


def shards(plus_counts, report_counts, clip_bounds):
    rows, middle, trailing = plus_counts.shape
    n = lax.axis_size("wide")
    chunks, tall = rows // CHUNK, CHUNK * middle
    groups = CHUNK // PAIR
    per_group = n // groups
    width = trailing // per_group
    piece = (PAIR * middle, width)
    summed = pl.pallas_call(
        functools.partial(exchange, n),
        out_shape=jax.ShapeDtypeStruct((chunks, groups, per_group) + piece, jnp.bfloat16),
        in_specs=[
            pl.BlockSpec(memory_space=pl.ANY),
            pl.BlockSpec(memory_space=pl.ANY),
            pl.BlockSpec(memory_space=pltpu.VMEM),
        ],
        out_specs=pl.BlockSpec(memory_space=pl.ANY),
        scratch_shapes=[
            pltpu.VMEM((FACTOR, FACTOR), jnp.bfloat16),
            pltpu.VMEM((tall, tall), jnp.bfloat16),
            pltpu.VMEM((2, tall, trailing), jnp.int32),
            pltpu.VMEM((2, tall, trailing), jnp.int32),
            pltpu.VMEM((tall, trailing), jnp.float32),
            pltpu.VMEM((chunks, groups, per_group) + piece, jnp.bfloat16),
            pltpu.VMEM((chunks, n) + piece, jnp.bfloat16),
            pltpu.VMEM((chunks, n) + piece, jnp.bfloat16),
            pltpu.SemaphoreType.DMA((2, 2)),
            pltpu.SemaphoreType.DMA((chunks,)),
            pltpu.SemaphoreType.DMA((chunks,)),
            pltpu.SemaphoreType.DMA((chunks,)),
            pltpu.SemaphoreType.DMA((chunks,)),
            pltpu.SemaphoreType.DMA((chunks,)),
        ],
        compiler_params=pltpu.CompilerParams(
            collective_id=0, has_side_effects=True, vmem_limit_bytes=56 * 1024 * 1024
        ),
    )(
        plus_counts.reshape(chunks, tall, trailing),
        report_counts.reshape(chunks, tall, trailing),
        clip_bounds,
    )
    wide = 256
    inside = width // wide
    return pl.pallas_call(
        leading,
        grid=(trailing // wide,),
        out_shape=jax.ShapeDtypeStruct((rows, middle, trailing), jnp.float32),
        in_specs=[
            pl.BlockSpec((chunks, groups, 1, PAIR * middle, wide), lambda c: (0, 0, c // inside, 0, c % inside))
        ],
        out_specs=pl.BlockSpec((rows, middle, wide), lambda c: (0, 0, c)),
        compiler_params=pltpu.CompilerParams(vmem_limit_bytes=32 * 1024 * 1024),
    )(summed)


def solution(mesh):
    placed = (
        P(("groups", "wide"), None, None),
        P(("groups", "wide"), None, None),
        P(("groups", "wide"), None),
    )
    return jax.shard_map(
        shards,
        mesh=mesh,
        in_specs=placed,
        out_specs=P(("groups", "wide"), None, None),
        check_vma=False,
    )
```

time: 738 us -> 390 us (0.53)
  blocking collectives: 398 us -> 0 us
  Pallas kernels: 0 us -> 380 us
  local copies, waits for them, and re-layouts: 162 us -> 4.86 us
  matrix products: 95.5 us -> 0 us
  waiting for transfers between devices: 43.4 us -> 0 us
  other arithmetic: 27.9 us -> 0 us
    all_to_all x1 -> x0, blocking collectives: 398 us -> none  [shards(): lax.all_to_all(decoded, 'wide', split_axis=0, concat_axis=2, tiled=True)]
    pallas_call x0 -> x2, Pallas kernels: none -> 380 us  [the longest x1 363 us: shards(): pl.pallas_call(functools.partial(exchange, n), out_shape=jax.ShapeDtypeSt...]
    mul x2 -> x0, local copies, waits for them, and re-layouts: 110 us -> none  [kron_hadamard(): left[:, None, :, None] * right[None, :, None, :]]
    dot_general x3 -> x0, matrix products: 95.5 us -> none  [the longest x1 42.4 us: shards(): jnp.dot(hadamard_a, regrouped.reshape(leading, -1), preferred_element_typ...]
    all_to_all x1 -> x0, waiting for transfers between devices: 43.4 us -> none  [shards(): lax.all_to_all(mixed, 'wide', split_axis=2, concat_axis=0, tiled=True)]
    mul x2 -> x0, other arithmetic: 27.2 us -> none  [kron_hadamard(): left[:, None, :, None] * right[None, :, None, :]]
    all_to_all x2 -> x0, local copies, waits for them, and re-layouts: 19.7 us -> none  [the longest x1 13.2 us: shards(): lax.all_to_all(mixed, 'wide', split_axis=2, concat_axis=0, tiled=True)]
    reshape x1 -> x0, local copies, waits for them, and re-layouts: 17.5 us -> none  [shards(): decoded = (outer * (1.0 / 64.0)).reshape(leading, width_mid, -1)]
  transfers between devices with their start and end apart: 1 -> 0, of which waited for: 1 -> 0; matrix products, arithmetic and copies ran while one was open for 15% -> 0% of each run, Pallas kernels for 0% -> 0%
where the time goes in v1:
time: 390 us; the launch traced here: 384 us
  Pallas kernels  380 us (97%)
  local copies, waits for them, and re-layouts  4.86 us (1%)
    pallas_call x1, Pallas kernels, shards(): pl.pallas_call(functools.partial(exchange, n), out_shape=jax.ShapeDtypeSt...  363 us
    pallas_call x1, Pallas kernels, shards(): pl.pallas_call(leading, grid=(trailing // wide,), out_shape=jax.ShapeDtyp...  16.4 us

profile of v1, /device:TPU:1, one launch (start us, length us, event | category | flops | bytes accessed | tf_op | source)
XLA Modules:
  0.0 384.4 jit_solution(3946706863163270583)
XLA Ops:
  0.0 1.5 copy.4.bound_ref
  1.5 363.2 %shard_map.37.summed_ref = bf16[8,16,1,16,2048]{4,3,2,1,0:T(8,128)(2,1)} custom-call(s32[8,256,2048]{2,1,0:T(8,128)} %bitcast.2, s32[8,256,2048]{2,1,0:T(8,128)} %bitcast.3, s32[256,8]{1,0:T(8,128)} %copy.4.bound_ref), custom_call_target="tpu_custom_call" | custom-call | tf_op jit(solution)/shard_map/pallas_call | solution.py:222
  364.7 0.0 copy-start
  364.7 3.4 copy-done
  368.1 16.4 %shard_map.38 = f32[256,8,2048]{2,1,0:T(8,128)} custom-call(bf16[8,16,1,16,2048]{4,3,2,1,0:T(8,128)(2,1)S(1)} %copy-done), custom_call_target="tpu_custom_call" | custom-call | tf_op jit(solution)/shard_map/pallas_call | solution.py:257
Async XLA Ops:
  364.7 3.4 copy-start

commit v2 on v1

--- a/solution.py
+++ b/solution.py
@@ -33,9 +33,22 @@
     return (1 - 2 * (both & 1)).astype(jnp.float32)
 
 
+def order(turn, n):
+    later = lax.rem(turn, 2)
+    return n - 1 - lax.div(turn, 2) - later * (n // 2)
+
+
+def partner(me, other, n):
+    bit, found = 1, 0
+    while bit < n:
+        found = found + lax.rem(lax.div(me, bit) + (other // bit), 2) * bit
+        bit *= 2
+    return found
+
+
 def exchange(
     n, plus_ref, report_ref, bound_ref, out_ref,
-    had_b, had_c, plus_buf, report_buf, inner, mixed, got, summed,
+    had_b, had_c, bounds, plus_buf, report_buf, inner, mixed, got, summed,
     load_sem, send_one, recv_one, send_two, recv_two, own_sem,
 ):
     me = lax.axis_index("wide")
@@ -67,8 +80,13 @@
     had_b[...] = signs(row & col).astype(jnp.bfloat16)
     row = lax.broadcasted_iota(jnp.int32, (tall, tall), 0)
     col = lax.broadcasted_iota(jnp.int32, (tall, tall), 1)
-    near = (row ^ col) < middle
-    had_c[...] = jnp.where(near, signs(row & col & (middle - 1)), 0.0).astype(jnp.bfloat16)
+    had_c[...] = signs(row & col).astype(jnp.bfloat16)
+    turned = (row == col).astype(jnp.float32).astype(jnp.bfloat16)
+    for k in range(chunks):
+        part = bound_ref[...] if chunks == 1 else bound_ref[:, k * CHUNK : (k + 1) * CHUNK]
+        bounds[pl.ds(k * CHUNK, CHUNK), :] = lax.dot_general(
+            turned[:CHUNK, :CHUNK], part.astype(jnp.float32).astype(jnp.bfloat16),
+            (((1,), (1,)), ((), ())), preferred_element_type=jnp.float32)
 
     pl.semaphore_wait(barrier, n - 1)
 
@@ -82,11 +100,11 @@
 
         for load in loads(k):
             load.wait()
-        bounds = bound_ref[pl.ds(pl.multiple_of(k * CHUNK, CHUNK), CHUNK), :]
-        bounds = jnp.broadcast_to(bounds[:, None, :], (CHUNK, middle, middle)).reshape(tall, middle)
+        each = bounds[pl.ds(pl.multiple_of(k * CHUNK, CHUNK), CHUNK), :]
+        each = jnp.broadcast_to(each[:, None, :], (CHUNK, middle, middle)).reshape(tall, middle)
         pick = lax.broadcasted_iota(jnp.int32, (tall, middle), 0) % middle
         pick = pick == lax.broadcasted_iota(jnp.int32, (tall, middle), 1)
-        bound = jnp.sum(jnp.where(pick, bounds.astype(jnp.float32), 0.0), axis=1, keepdims=True)
+        bound = jnp.sum(jnp.where(pick, each, 0.0), axis=1, keepdims=True)
         for block in range(blocks):
             cols = pl.ds(block * FACTOR, FACTOR)
             plus = plus_buf[slot, :, cols]
@@ -114,8 +132,9 @@
             mixed[k, :, part, :, pl.ds(start, FACTOR)] = done.reshape(-1, PAIR * middle, FACTOR)
         got[k, 0] = mixed[k, lax.div(me, per_group), lax.rem(me, per_group)]
 
-        def send(step, carry):
-            to = lax.rem(me + step, n)
+        def send(turn, carry):
+            step = order(turn, n)
+            to = partner(me, step, n)
             pltpu.make_async_remote_copy(
                 src_ref=mixed.at[k, lax.div(to, per_group), lax.rem(to, per_group)],
                 dst_ref=got.at[k, step],
@@ -126,7 +145,7 @@
             ).start()
             return carry
 
-        lax.fori_loop(1, n, send, 0)
+        lax.fori_loop(0, n - 1, send, 0)
         return carry
 
     lax.fori_loop(0, chunks, front, 0)
@@ -145,7 +164,7 @@
 
         def strip(tile, carry):
             cols = pl.ds(pl.multiple_of(tile * LANES, LANES), LANES)
-            parts = [got[k, lax.rem(me + (n - source), n), :, cols].astype(jnp.float32) for source in range(n)]
+            parts = [got[k, partner(me, source, n), :, cols].astype(jnp.float32) for source in range(n)]
             parts = butterfly(parts)
             for to in range(n):
                 summed[k, to, :, cols] = (parts[to] * (1.0 / 64.0)).astype(jnp.bfloat16)
@@ -154,8 +173,9 @@
         lax.fori_loop(0, width // LANES, strip, 0)
         own(k).start()
 
-        def send(step, carry):
-            to = lax.rem(me + step, n)
+        def send(turn, carry):
+            step = order(turn, n)
+            to = partner(me, step, n)
             pltpu.make_async_remote_copy(
                 src_ref=summed.at[k, to],
                 dst_ref=out_ref.at[k, lax.div(me, per_group), lax.rem(me, per_group)],
@@ -166,7 +186,7 @@
             ).start()
             return carry
 
-        lax.fori_loop(1, n, send, 0)
+        lax.fori_loop(0, n - 1, send, 0)
         return carry
 
     lax.fori_loop(0, chunks, combine, 0)
@@ -184,31 +204,16 @@
 def leading(summed_ref, out_ref):
     rows, middle, wide = out_ref.shape
     chunks, groups = summed_ref.shape[:2]
-    tiles = wide // LANES
-    per_chunk = CHUNK // RADIX
-
-    def inside(index, carry):
-        block, tile = index // tiles, index % tiles
-        cols = pl.ds(pl.multiple_of(tile * LANES, LANES), LANES)
-        group = pl.ds((block % per_chunk) * (RADIX // PAIR), RADIX // PAIR)
-        parts = summed_ref[block // per_chunk, group, 0, :, cols].astype(jnp.float32)
-        parts = parts.reshape(RADIX, middle, LANES)
-        parts = butterfly([parts[i] for i in range(RADIX)])
-        for i in range(RADIX):
-            out_ref[block * RADIX + i, :, cols] = parts[i]
-        return carry
-
-    lax.fori_loop(0, rows // RADIX * tiles, inside, 0)
-
-    def across(index, carry):
-        low, tile = index // tiles, index % tiles
-        cols = pl.ds(pl.multiple_of(tile * LANES, LANES), LANES)
-        parts = butterfly([out_ref[high * RADIX + low, :, cols] for high in range(rows // RADIX)])
-        for high in range(rows // RADIX):
-            out_ref[high * RADIX + low, :, cols] = parts[high]
-        return carry
-
-    lax.fori_loop(0, RADIX * tiles, across, 0)
+
+    def inside(group, carry):
+        for tile in range(wide // LANES):
+            cols = pl.ds(tile * LANES, LANES)
+            parts = butterfly([summed_ref[k, group, 0, :, cols].astype(jnp.float32) for k in range(chunks)])
+            for k in range(chunks):
+                out_ref[pl.ds(k * CHUNK + group * PAIR, PAIR), :, cols] = parts[k].reshape(PAIR, middle, LANES)
+        return carry
+
+    lax.fori_loop(0, groups, inside, 0)
 
 
 def shards(plus_counts, report_counts, clip_bounds):
@@ -231,6 +236,7 @@
         scratch_shapes=[
             pltpu.VMEM((FACTOR, FACTOR), jnp.bfloat16),
             pltpu.VMEM((tall, tall), jnp.bfloat16),
+            pltpu.VMEM((rows, middle), jnp.float32),
             pltpu.VMEM((2, tall, trailing), jnp.int32),
             pltpu.VMEM((2, tall, trailing), jnp.int32),
             pltpu.VMEM((tall, trailing), jnp.float32),
@@ -245,12 +251,12 @@
             pltpu.SemaphoreType.DMA((chunks,)),
         ],
         compiler_params=pltpu.CompilerParams(
-            collective_id=0, has_side_effects=True, vmem_limit_bytes=56 * 1024 * 1024
+            collective_id=0, has_side_effects=True, vmem_limit_bytes=42 * 1024 * 1024
         ),
     )(
         plus_counts.reshape(chunks, tall, trailing),
         report_counts.reshape(chunks, tall, trailing),
-        clip_bounds,
+        clip_bounds.T,
     )
     wide = 256
     inside = width // wide
@@ -262,7 +268,7 @@
             pl.BlockSpec((chunks, groups, 1, PAIR * middle, wide), lambda c: (0, 0, c // inside, 0, c % inside))
         ],
         out_specs=pl.BlockSpec((rows, middle, wide), lambda c: (0, 0, c)),
-        compiler_params=pltpu.CompilerParams(vmem_limit_bytes=32 * 1024 * 1024),
+        compiler_params=pltpu.CompilerParams(vmem_limit_bytes=42 * 1024 * 1024),
     )(summed)
 
 

time: 390 us -> 379 us (0.972); the launches traced: 384 us -> 378 us
  local copies, waits for them, and re-layouts: 4.86 us -> 0.7 us
    pallas_call x1, Pallas kernels: 16.4 us -> 8.13 us  [shards(): pl.pallas_call(leading, grid=(trailing // wide,), out_shape=jax.ShapeDtyp...]
    pallas_call x1, Pallas kernels: 363 us -> 369 us  [shards(): pl.pallas_call(functools.partial(exchange, n), out_shape=jax.ShapeDtypeSt...]
    unnamed x3 -> x2, local copies, waits for them, and re-layouts: 4.86 us -> 0.7 us
where the time goes in v2:
time: 379 us; the launch traced here: 378 us
  Pallas kernels  377 us (99%)
    pallas_call x1, Pallas kernels, shards(): pl.pallas_call(functools.partial(exchange, n), out_shape=jax.ShapeDtypeSt...  369 us
    pallas_call x1, Pallas kernels, shards(): pl.pallas_call(leading, grid=(trailing // wide,), out_shape=jax.ShapeDtyp...  8.13 us

profile of v2, /device:TPU:1, one launch (start us, length us, event | category | flops | bytes accessed | tf_op | source)
XLA Modules:
  0.0 377.8 jit_solution(923643794192579047)
XLA Ops:
  0.0 0.0 copy-start
  0.0 0.7 copy-done
  0.7 369.0 %shard_map.37.summed_ref = bf16[8,16,1,16,2048]{4,3,2,1,0:T(8,128)(2,1)S(1)} custom-call(s32[8,256,2048]{2,1,0:T(8,128)} %bitcast.4, s32[8,256,2048]{2,1,0:T(8,128)} %bitcast.5, s32[8,256]{1,0:T(8,128)S(1)} %bitcast.3), custom_call_target="tpu_custom_call" | custom-call | tf_op jit(solution)/shard_map/pallas_call | solution.py:227
  369.7 8.1 %shard_map.38 = f32[256,8,2048]{2,1,0:T(8,128)} custom-call(bf16[8,16,1,16,2048]{4,3,2,1,0:T(8,128)(2,1)S(1)} %shard_map.37.summed_ref), custom_call_target="tpu_custom_call" | custom-call | tf_op jit(solution)/shard_map/pallas_call | solution.py:263
Async XLA Ops:
  0.0 0.7 copy-start
